TPU v7x, 512 devices: a whole 4x8x8 slice. The times are simulated.
512 devices in a mesh: space: 64 (over z, y), tensor: 8 (over x, core).
Axes of the slice: x: 4, y: 8, z: 8, core: 2. Of those that a mesh axis runs over, the one named last changes fastest.
Arguments:
- tokens: bfloat16 [57344, 1024], P('space', 'tensor'), may hold values from -16 to 16
- first_weight: bfloat16 [1024, 1024], P(None, 'tensor'), may hold values from -0.1875 to 0.1875
- second_weight: bfloat16 [1024, 1024], P(None, 'tensor'), may hold values from -0.1875 to 0.1875
- head_weight: bfloat16 [352, 1024], P('tensor'), may hold values from -0.1875 to 0.1875
- targets: float32 [352, 57344], P('tensor', 'space'), may hold values from -6 to 6
- land_mask: int32 [4, 57344], P(None, 'space'), may hold values from 0 to 1, as said below
- variable_kind: int32 [88], P('tensor'), may hold values from 0 to 2
- loss_scale: float32 [], replicated, may hold values from 2523136 to 20185088
Outputs:
- loss: float32 [], replicated
- token_grad: float32 [57344, 1024], P('space', 'tensor')
- first_grad: float32 [1024, 1024], P('space', 'tensor')
- second_grad: float32 [1024, 1024], P('space', 'tensor')
- head_grad: float32 [352, 1024], P('tensor', 'space')
Inputs may be any that keep to these rules, and one draw needn't show every extreme that they name: `land_mask`: every aligned group of 8 entries along the last dimension holds at least one 1 and one 0. `variable_kind`: 0 scores a variable on all cells, 1 on land cells, 2 on ocean cells.
All inputs are finite; a program needn't handle non-finite values.
Results may differ from a plain program's by a relative error of at most 0.0056.
Values may be sent and summed in bfloat16 or wider, within the bound.
No kernel may reach another device: no remote copies, remote signals or barrier semaphores. Data moves between devices by JAX's collectives and lax.ppermute only.
A program may use at most 64 MiB of HBM per device.

v0:
```python
import math
import jax
import jax.numpy as jnp
from jax import lax
from jax.sharding import PartitionSpec as P

V = 88
PP = 4
PROW_DEV = 4
LONP = 224


def sent_to_all(shard, axis):
    copies = jnp.broadcast_to(shard, (lax.axis_size(axis), *shard.shape))
    return lax.all_to_all(copies, axis, split_axis=0, concat_axis=0, tiled=True)


def over_copies(shard, axis):
    everything = sent_to_all(shard, axis)
    return jnp.sum(everything, axis=0)


def split_up(shard, dim, size):
    before, after = (shard.shape[:dim], shard.shape[dim + 1 :])
    return jnp.moveaxis(shard.reshape(*before, size, -1, *after), dim, 0)


def sent_and_summed(shard, axis, dim):
    size = lax.axis_size(axis)
    parts = lax.all_to_all(split_up(shard, dim, size), axis, 0, 0, tiled=True)
    return jnp.sum(parts, axis=0)


def laid_out(parts, dim):
    parts = jnp.moveaxis(parts, 0, dim)
    lengths = parts.shape
    return parts.reshape(*lengths[:dim], lengths[dim] * lengths[dim + 1], *lengths[dim + 2 :])


def gather_directly(shard, axis, dim):
    parts = sent_to_all(shard, axis)
    return laid_out(parts, dim)


def sum_at_owner(shard, axis, dim):
    parts = split_up(shard, dim, lax.axis_size(axis))
    arrived = lax.all_to_all(parts, axis, split_axis=0, concat_axis=0, tiled=True)
    return arrived.astype(jnp.float32).sum(axis=0)


def slope(z):
    cdf = 0.5 * (1.0 + lax.erf(z / math.sqrt(2.0)))
    return cdf + z * jnp.exp(-0.5 * z * z) / math.sqrt(2.0 * math.pi)


def column_folder(weights, piece):
    return lax.dot_general(
        piece, weights, (((1,), (1,)), ((), ())), preferred_element_type=jnp.float32
    )


def row_folder(weights, piece):
    return lax.dot_general(
        piece, weights, (((0,), (0,)), ((), ())), preferred_element_type=jnp.float32
    )


def per_device(
    tokens, first_weight, second_weight, head_weight, targets, land_mask, variable_kind, loss_scale
):
    count = tokens.shape[0]
    width = first_weight.shape[1]
    kinds = head_weight.shape[0] // PP
    rows_first, rows_second = (
        lax.all_to_all(first_weight, "tensor", split_axis=0, concat_axis=1, tiled=True),
        lax.all_to_all(second_weight, "tensor", split_axis=0, concat_axis=1, tiled=True),
    )
    head_cols = lax.all_to_all(head_weight, "tensor", split_axis=1, concat_axis=0, tiled=True)
    position = lax.axis_index("space") * count + jnp.arange(count, dtype=jnp.int32)
    cell = jnp.arange(PP, dtype=jnp.int32)
    lat_row = 2 * (position // LONP)[None, :] + (cell // 2)[:, None]
    nlat = 2 * PROW_DEV * lax.axis_size("space")
    cell_weight = jnp.cos(math.pi / 2.0 * (lat_row.astype(jnp.float32) + 0.5) / nlat)
    land = land_mask.astype(jnp.float32)
    kind = variable_kind[:, None, None]
    valid = jnp.where(kind == 0, 1.0, jnp.where(kind == 1, land[None], 1.0 - land[None]))
    masked = cell_weight[None] * valid
    local_weight = jnp.sum(masked, axis=(1, 2))
    weight_sum = over_copies(local_weight, "space")
    full_in = lax.all_gather(tokens, "tensor", axis=1, tiled=True)
    pre_one = jnp.dot(full_in, first_weight, preferred_element_type=jnp.float32)
    hidden_one = jax.nn.gelu(pre_one, approximate=False).astype(jnp.bfloat16)
    full_one = lax.all_gather(hidden_one, "tensor", axis=1, tiled=True)
    pre_two = jnp.dot(full_one, second_weight, preferred_element_type=jnp.float32)
    hidden_two = jax.nn.gelu(pre_two, approximate=False).astype(jnp.bfloat16)
    full_two = lax.all_gather(hidden_two, "tensor", axis=1, tiled=True)
    predicted = lax.dot_general(
        head_weight, full_two, (((1,), (1,)), ((), ())), preferred_element_type=jnp.float32
    )
    error = predicted.reshape(kinds, PP, count) - targets.reshape(kinds, PP, count)
    local_error = jnp.sum(masked * error * error, axis=(1, 2))
    error_sum = over_copies(local_error, "space")
    root = jnp.sqrt(error_sum / weight_sum + 1e-06)
    loss = lax.psum(jnp.sum(root), "tensor") / V
    coef = loss_scale / (V * root * weight_sum)
    grad_pred = (
        (coef[:, None, None] * masked * error).reshape(kinds * PP, count).astype(jnp.bfloat16)
    )
    back_two = row_folder(head_cols, lax.all_gather(grad_pred, "tensor", axis=0, tiled=True))
    head_term = jnp.dot(grad_pred, full_two, preferred_element_type=jnp.float32)
    head_grad = sent_and_summed(head_term, "space", 1)
    grad_two = (back_two * slope(pre_two)).astype(jnp.bfloat16)
    back_one = column_folder(rows_second, gather_directly(grad_two, "tensor", 1))
    grad_one = (back_one * slope(pre_one)).astype(jnp.bfloat16)
    joined = sum_at_owner(
        jnp.concatenate(
            [
                lax.dot_general(
                    full_one, grad_two, (((0,), (0,)), ((), ())), preferred_element_type=jnp.float32
                ),
                lax.dot_general(
                    full_in, grad_one, (((0,), (0,)), ((), ())), preferred_element_type=jnp.float32
                ),
            ],
            axis=1,
        ).astype(jnp.bfloat16),
        "space",
        0,
    )
    second_grad = joined[:, :width]
    first_grad = joined[:, width:]
    token_grad = column_folder(rows_first, lax.all_gather(grad_one, "tensor", axis=1, tiled=True))
    return (loss, token_grad, first_grad, second_grad, head_grad)


def solution(mesh):
    return jax.shard_map(
        per_device,
        mesh=mesh,
        in_specs=(
            P("space", "tensor"),
            P(None, "tensor"),
            P(None, "tensor"),
            P("tensor", None),
            P("tensor", "space"),
            P(None, "space"),
            P("tensor"),
            P(),
        ),
        out_specs=(
            P(),
            P("space", "tensor"),
            P("space", "tensor"),
            P("space", "tensor"),
            P("tensor", "space"),
        ),
        check_vma=False,
    )
```

profile of v0, /device:TPU:4, one launch (start us, length us, event | category | flops | bytes accessed | tf_op | source)
XLA Modules:
  0.0 263.3 jit_solution(2993436347642144659)
XLA Ops:
  7.2 0.7 all-gather.6.cloned.1.call-update
  7.9 38.0 %all-gather.6.cloned.1.call-done = bf16[896,1024]{1,0:T(8,128)(2,1)} async-done(((bf16[896,128]{1,0:T(8,128)(2,1)}), bf16[896,1024]{1,0:T(8,128)(2,1)}) %all-gather.6.cloned.1.call-update) | async-done | bytes 1835024 | tf_op jit(solution)/shard_map/all_gather | solution.py:90
  46.0 3.6 %fusion.21 = (bf16[896,128]{1,0:T(8,128)(2,1)}, f32[896,128]{1,0:T(8,128)S(1)}) fusion(bf16[896,1024]{1,0:T(8,128)(2,1)} %all-gather.6.cloned.1.call-done, bf16[1024,128]{1,0:T(8,128)(2,1)} %param.9), kind=kOutput, calls=%fused_computation.23 | convolution fusion | flops 242335744 | bytes 2785280 | tf_op jit(solution)/shard_map/dot_general | solution.py:91
  49.7 32.6 %all-gather.8.cloned.1.call-done = bf16[896,1024]{1,0:T(8,128)(2,1)} async-done(((bf16[896,128]{1,0:T(8,128)(2,1)}), bf16[896,1024]{1,0:T(8,128)(2,1)}) %all-gather.8.cloned.1.call-update) | async-done | bytes 1835024 | tf_op jit(solution)/shard_map/all_gather | solution.py:93
  82.3 3.6 %fusion.24 = (bf16[896,128]{1,0:T(8,128)(2,1)}, f32[896,128]{1,0:T(8,128)S(1)}) fusion(bf16[896,1024]{1,0:T(8,128)(2,1)} %all-gather.8.cloned.1.call-done, bf16[1024,128]{1,0:T(8,128)(2,1)} %param.10), kind=kOutput, calls=%fused_computation.26 | convolution fusion | flops 242335744 | bytes 2785280 | tf_op jit(solution)/shard_map/dot_general | solution.py:94
  86.5 0.6 broadcast_in_dim.85
  87.1 13.3 %all-to-all-start.1 = ((f32[64,1,11]{2,1,0:T(1,128)}), f32[64,1,11]{2,1,0:T(1,128)S(1)}, u32[]{:S(2)}, u32[]{:S(2)}) async-start(f32[64,1,11]{2,1,0:T(1,128)} %broadcast_in_dim.85), calls=%async_computation.1 | async-start | bytes 65536 | tf_op jit(solution)/shard_map/all_to_all | solution.py:15
  100.8 0.7 copy.46
  101.7 10.7 %all-to-all-done.1 = f32[64,1,11]{2,1,0:T(1,128)S(1)} async-done(((f32[64,1,11]{2,1,0:T(1,128)}), f32[64,1,11]{2,1,0:T(1,128)S(1)}, u32[]{:S(2)}, u32[]{:S(2)}) %all-to-all-start.1) | async-done | bytes 2848 | tf_op jit(solution)/shard_map/all_to_all | solution.py:15
  112.4 4.8 %all-to-all-start.2 = ((bf16[44,8,128]{2,0,1:T(8,128)(2,1)}), bf16[44,8,128]{2,0,1:T(8,128)(2,1)S(1)}, u32[]{:S(2)}, u32[]{:S(2)}) async-start(bf16[44,8,128]{2,0,1:T(8,128)(2,1)} %copy.46), calls=%async_computation.2 | async-start | bytes 196608 | tf_op jit(solution)/shard_map/all_to_all | solution.py:78
  117.2 1.4 all-gather.10.cloned.1.call-done
  118.6 2.3 fusion.48
  121.7 13.9 %all-to-all-start = ((f32[64,1,11]{2,1,0:T(1,128)}), f32[64,1,11]{2,1,0:T(1,128)S(1)}, u32[]{:S(2)}, u32[]{:S(2)}) async-start(f32[64,1,11]{2,1,0:T(1,128)} %broadcast_in_dim.81), calls=%async_computation | async-start | bytes 65536 | tf_op jit(solution)/shard_map/all_to_all | solution.py:15
  136.4 11.2 %all-to-all-done = f32[64,1,11]{2,1,0:T(1,128)S(1)} async-done(((f32[64,1,11]{2,1,0:T(1,128)}), f32[64,1,11]{2,1,0:T(1,128)S(1)}, u32[]{:S(2)}, u32[]{:S(2)}) %all-to-all-start) | async-done | bytes 2848 | tf_op jit(solution)/shard_map/all_to_all | solution.py:15
  147.5 4.9 %all-to-all-start.4 = ((bf16[8,128,128]{2,1,0:T(8,128)(2,1)}), bf16[8,128,128]{2,1,0:T(8,128)(2,1)S(1)}, u32[]{:S(2)}, u32[]{:S(2)}) async-start(bf16[8,128,128]{2,1,0:T(8,128)(2,1)} %bitcast.4), calls=%async_computation.4 | async-start | bytes 524288 | tf_op jit(solution)/shard_map/all_to_all | solution.py:76
  152.8 13.1 %all-gather = bf16[8,44,896]{2,1,0:T(8,128)(2,1)S(1)} all-gather(bf16[1,44,896]{2,1,0:T(8,128)(2,1)S(1)} %bitcast.69), channel_id=1, replica_groups=mesh['space'=64,'tensor'=8] {'tensor'}, dimensions={0}, use_global_device_ids=true | all-gather | bytes 709632 | tf_op jit(solution)/shard_map/all_gather | solution.py:109
  166.7 26.1 %all_to_all.81 = bf16[8,896,128]{2,1,0:T(8,128)(2,1)S(1)} all-to-all(bf16[8,896,128]{2,1,0:T(8,128)(2,1)S(1)} %broadcast_in_dim.86), channel_id=1, replica_groups=mesh['space'=64,'tensor'=8] {'tensor'}, dimensions={0} | all-to-all | bytes 3670016 | tf_op jit(solution)/shard_map/all_to_all | solution.py:15
  192.8 1.3 fusion.13
  194.1 6.5 %all-to-all-start.5 = ((bf16[8,128,128]{2,1,0:T(8,128)(2,1)}), bf16[8,128,128]{2,1,0:T(8,128)(2,1)S(1)}, u32[]{:S(2)}, u32[]{:S(2)}) async-start(bf16[8,128,128]{2,1,0:T(8,128)(2,1)} %bitcast.7), calls=%async_computation.5 | async-start | bytes 524288 | tf_op jit(solution)/shard_map/all_to_all | solution.py:75
  200.6 2.5 copy.49
  203.1 2.6 fusion.7
  206.1 1.2 reshape.129
  207.3 2.2 convolution_convert_fusion.1
  209.5 4.8 %all-to-all-start.7 = ((f32[64,1,704]{2,1,0:T(1,128)}), f32[64,1,704]{2,1,0:T(1,128)S(1)}, u32[]{:S(2)}, u32[]{:S(2)}) async-start(f32[64,1,704]{2,1,0:T(1,128)} %reshape.129), calls=%async_computation.7 | async-start | bytes 393216 | tf_op jit(solution)/shard_map/all_to_all | solution.py:30
  215.0 0.9 pad_maximum_fusion
  215.8 12.9 %all-to-all-done.7 = f32[64,1,704]{2,1,0:T(1,128)S(1)} async-done(((f32[64,1,704]{2,1,0:T(1,128)}), f32[64,1,704]{2,1,0:T(1,128)S(1)}, u32[]{:S(2)}, u32[]{:S(2)}) %all-to-all-start.7) | async-done | bytes 180256 | tf_op jit(solution)/shard_map/all_to_all | solution.py:30
  228.7 4.6 %all-to-all-start.6 = ((bf16[64,16,256]{2,1,0:T(8,128)(2,1)}), bf16[64,16,256]{2,1,0:T(8,128)(2,1)S(1)}, u32[]{:S(2)}, u32[]{:S(2)}) async-start(bf16[64,16,256]{2,1,0:T(8,128)(2,1)} %pad_maximum_fusion), calls=%async_computation.6 | async-start | bytes 1048576 | tf_op jit(solution)/shard_map/all_to_all | solution.py:47
  234.1 11.2 %psum.7 = f32[]{:T(128)} all-reduce(f32[]{:T(128)} %reduce_sum.76), channel_id=1, replica_groups=mesh['space'=64,'tensor'=8] {'tensor'}, use_global_device_ids=true, to_apply=%region_6.7 | all-reduce | flops 1 | bytes 8 | tf_op jit(solution)/shard_map/psum | solution.py:104
  246.5 1.1 reduce.4
  248.0 0.7 bitcast_reduce_fusion
  248.7 3.3 %all-to-all-done.6 = bf16[64,16,256]{2,1,0:T(8,128)(2,1)S(1)} async-done(((bf16[64,16,256]{2,1,0:T(8,128)(2,1)}), bf16[64,16,256]{2,1,0:T(8,128)(2,1)S(1)}, u32[]{:S(2)}, u32[]{:S(2)}) %all-to-all-start.6) | async-done | bytes 524320 | tf_op jit(solution)/shard_map/all_to_all | solution.py:47
  252.7 2.9 %fusion.53 = f32[896,128]{1,0:T(8,128)} fusion(bf16[896,1024]{1,0:T(8,128)(2,1)} %all-gather.12.cloned.1.call-done, bf16[128,1024]{0,1:T(8,128)(2,1)S(1)} %bitcast.62), kind=kOutput, calls=%fused_computation.90 | convolution fusion | flops 234881024 | bytes 2555904 | tf_op jit(solution)/shard_map/dot_general | solution.py:57
  (65 shorter events, 6.7 us)
Async XLA Ops:
  7.2 38.8 %all-gather.6.cloned.1.call-start = ((), (), s32[]{:S(2)}) async-start(), calls=%async_computation.8 | async-start | bytes 2064384 | tf_op jit(solution)/shard_map/all_gather | solution.py:90
  7.9 74.4 %all-gather.8.cloned.1.call-start = ((), (), s32[]{:S(2)}) async-start(), calls=%async_computation.9 | async-start | bytes 2064384 | tf_op jit(solution)/shard_map/all_gather | solution.py:93
  49.6 36.3 %copy-start.5 = (s32[4,896]{1,0:T(4,128)S(1)}, s32[4,896]{1,0:T(4,128)}, u32[]{:S(2)}) copy-start(s32[4,896]{1,0:T(4,128)} %param.13) | copy-start | bytes 43012
  49.6 36.4 %copy-start.6 = (s32[11]{0:T(128)S(1)}, s32[11]{0:T(128)}, u32[]{:S(2)}) copy-start(s32[11]{0:T(128)} %param.14) | copy-start | bytes 136
  49.6 51.1 %copy-start.3 = (bf16[44,1024]{1,0:T(8,128)(2,1)S(1)}, bf16[44,1024]{1,0:T(8,128)(2,1)}, u32[]{:S(2)}) copy-start(bf16[44,1024]{1,0:T(8,128)(2,1)} %param.11) | copy-start | bytes 270340
  49.6 68.9 %all-gather.10.cloned.1.call-start = ((), (), s32[]{:S(2)}) async-start(), calls=%async_computation.10 | async-start | bytes 2064384 | tf_op jit(solution)/shard_map/all_gather | solution.py:96
  85.9 32.7 %copy-start.4 = (f32[44,896]{1,0:T(8,128)S(1)}, f32[44,896]{1,0:T(8,128)}, u32[]{:S(2)}) copy-start(f32[44,896]{1,0:T(8,128)} %param.12) | copy-start | bytes 473092
  87.1 25.3 %all-to-all-start.1 = ((f32[64,1,11]{2,1,0:T(1,128)}), f32[64,1,11]{2,1,0:T(1,128)S(1)}, u32[]{:S(2)}, u32[]{:S(2)}) async-start(f32[64,1,11]{2,1,0:T(1,128)} %broadcast_in_dim.85), calls=%async_computation.1 | async-start | bytes 65536 | tf_op jit(solution)/shard_map/all_to_all | solution.py:15
  112.4 8.7 %all-to-all-start.2 = ((bf16[44,8,128]{2,0,1:T(8,128)(2,1)}), bf16[44,8,128]{2,0,1:T(8,128)(2,1)S(1)}, u32[]{:S(2)}, u32[]{:S(2)}) async-start(bf16[44,8,128]{2,0,1:T(8,128)(2,1)} %copy.46), calls=%async_computation.2 | async-start | bytes 196608 | tf_op jit(solution)/shard_map/all_to_all | solution.py:78
  121.7 25.8 %all-to-all-start = ((f32[64,1,11]{2,1,0:T(1,128)}), f32[64,1,11]{2,1,0:T(1,128)S(1)}, u32[]{:S(2)}, u32[]{:S(2)}) async-start(f32[64,1,11]{2,1,0:T(1,128)} %broadcast_in_dim.81), calls=%async_computation | async-start | bytes 65536 | tf_op jit(solution)/shard_map/all_to_all | solution.py:15
  147.5 18.9 %all-to-all-start.4 = ((bf16[8,128,128]{2,1,0:T(8,128)(2,1)}), bf16[8,128,128]{2,1,0:T(8,128)(2,1)S(1)}, u32[]{:S(2)}, u32[]{:S(2)}) async-start(bf16[8,128,128]{2,1,0:T(8,128)(2,1)} %bitcast.4), calls=%async_computation.4 | async-start | bytes 524288 | tf_op jit(solution)/shard_map/all_to_all | solution.py:76
  152.4 100.3 %all-gather.12.cloned.1.call-start = ((), (), s32[]{:S(2)}) async-start(), calls=%async_computation.11 | async-start | bytes 2064384 | tf_op jit(solution)/shard_map/all_gather | solution.py:132
  192.8 7.9 %copy-start = (bf16[896,1024]{1,0:T(8,128)(2,1)S(1)}, bf16[896,1024]{1,0:T(8,128)(2,1)}, u32[]{:S(2)}) copy-start(bf16[896,1024]{1,0:T(8,128)(2,1)} %all-gather.10.cloned.1.call-done) | copy-start | bytes 5505028
  194.1 15.4 %all-to-all-start.5 = ((bf16[8,128,128]{2,1,0:T(8,128)(2,1)}), bf16[8,128,128]{2,1,0:T(8,128)(2,1)S(1)}, u32[]{:S(2)}, u32[]{:S(2)}) async-start(bf16[8,128,128]{2,1,0:T(8,128)(2,1)} %bitcast.7), calls=%async_computation.5 | async-start | bytes 524288 | tf_op jit(solution)/shard_map/all_to_all | solution.py:75
  206.0 8.3 %copy-start.1 = (bf16[896,1024]{1,0:T(8,128)(2,1)S(1)}, bf16[896,1024]{1,0:T(8,128)(2,1)}, u32[]{:S(2)}) copy-start(bf16[896,1024]{1,0:T(8,128)(2,1)} %all-gather.6.cloned.1.call-done) | copy-start | bytes 5505028
  206.1 8.3 %copy-start.2 = (bf16[896,128]{1,0:T(8,128)(2,1)S(1)}, bf16[896,128]{1,0:T(8,128)(2,1)}, u32[]{:S(2)}) copy-start(bf16[896,128]{1,0:T(8,128)(2,1)} %fusion.13) | copy-start | bytes 688132
  209.5 19.2 %all-to-all-start.7 = ((f32[64,1,704]{2,1,0:T(1,128)}), f32[64,1,704]{2,1,0:T(1,128)S(1)}, u32[]{:S(2)}, u32[]{:S(2)}) async-start(f32[64,1,704]{2,1,0:T(1,128)} %reshape.129), calls=%async_computation.7 | async-start | bytes 393216 | tf_op jit(solution)/shard_map/all_to_all | solution.py:30
  228.7 23.3 %all-to-all-start.6 = ((bf16[64,16,256]{2,1,0:T(8,128)(2,1)}), bf16[64,16,256]{2,1,0:T(8,128)(2,1)S(1)}, u32[]{:S(2)}, u32[]{:S(2)}) async-start(bf16[64,16,256]{2,1,0:T(8,128)(2,1)} %pad_maximum_fusion), calls=%async_computation.6 | async-start | bytes 1048576 | tf_op jit(solution)/shard_map/all_to_all | solution.py:47
Sparse Core Ops, SparseCore 0:
  10.1 35.7 all-gather.5
  49.7 32.4 all-gather.7
  86.0 32.4 all-gather.9
  194.2 25.7 all-gather.11
where the time goes:
time: 264 us; the launch traced here: 263 us
  waiting for transfers between devices  111 us (42%)
  starting transfers between devices  52.9 us (20%)
  blocking collectives  50.4 us (19%)
  matrix products  19.4 us (7%)
  between operations  16.5 us (6%)
  local copies, waits for them, and re-layouts  9 us (3%)
  other arithmetic  4.24 us (2%)
    all_gather x1, waiting for transfers between devices, per_device(): full_in = lax.all_gather(tokens, 'tensor', axis=1, tiled=True)  38 us
    all_gather x1, waiting for transfers between devices, per_device(): full_one = lax.all_gather(hidden_one, 'tensor', axis=1, tiled=True)  32.6 us
    all_to_all x2, starting transfers between devices, sent_to_all(): return lax.all_to_all(copies, axis, split_axis=0, concat_axis=0, tiled=True)  27.2 us
    all_to_all x1, blocking collectives, sent_to_all(): return lax.all_to_all(copies, axis, split_axis=0, concat_axis=0, tiled=True)  26.1 us
    all_to_all x2, waiting for transfers between devices, sent_to_all(): return lax.all_to_all(copies, axis, split_axis=0, concat_axis=0, tiled=True)  21.8 us
    all_gather x1, blocking collectives, per_device(): lax.all_gather(grad_pred, 'tensor', axis=0, tiled=True)  13.1 us
    all_to_all x1, waiting for transfers between devices, sent_and_summed(): parts = lax.all_to_all(split_up(shard, dim, size), axis, 0, 0, tiled=True)  12.9 us
    psum x1, blocking collectives, per_device(): loss = lax.psum(jnp.sum(root), 'tensor') / V  11.2 us
  transfers between devices with their start and end apart: 11, of which 7 were waited for; matrix products, arithmetic and copies ran while one was open for 8% of the time, Pallas kernels for 0%

commit v1 on v0

--- a/solution.py
+++ b/solution.py
@@ -75,7 +75,12 @@
         lax.all_to_all(first_weight, "tensor", split_axis=0, concat_axis=1, tiled=True),
         lax.all_to_all(second_weight, "tensor", split_axis=0, concat_axis=1, tiled=True),
     )
-    head_cols = lax.all_to_all(head_weight, "tensor", split_axis=1, concat_axis=0, tiled=True)
+    head_cols = jnp.concatenate(
+        lax.all_to_all(
+            jnp.stack(jnp.split(head_weight, lax.axis_size("tensor"), axis=1)), "tensor", 0, 0
+        ),
+        axis=0,
+    )
     position = lax.axis_index("space") * count + jnp.arange(count, dtype=jnp.int32)
     cell = jnp.arange(PP, dtype=jnp.int32)
     lat_row = 2 * (position // LONP)[None, :] + (cell // 2)[:, None]

time: 264 us -> 264 us (level)
  the two profiles are of different devices: /device:TPU:4 before, /device:TPU:2 now
where the time goes in v1:
time: 264 us; the launch traced here: 263 us
  waiting for transfers between devices  107 us (41%)
  blocking collectives  52.2 us (20%)
  starting transfers between devices  51.1 us (19%)
  matrix products  19.4 us (7%)
  between operations  16.5 us (6%)
  local copies, waits for them, and re-layouts  13.1 us (5%)
  other arithmetic  4.24 us (2%)
    all_gather x1, waiting for transfers between devices, per_device(): full_in = lax.all_gather(tokens, 'tensor', axis=1, tiled=True)  37.8 us
    all_gather x1, waiting for transfers between devices, per_device(): full_one = lax.all_gather(hidden_one, 'tensor', axis=1, tiled=True)  32.6 us
    all_to_all x1, blocking collectives, sent_to_all(): return lax.all_to_all(copies, axis, split_axis=0, concat_axis=0, tiled=True)  27.5 us
    all_to_all x2, starting transfers between devices, sent_to_all(): return lax.all_to_all(copies, axis, split_axis=0, concat_axis=0, tiled=True)  25.9 us
    all_to_all x2, waiting for transfers between devices, sent_to_all(): return lax.all_to_all(copies, axis, split_axis=0, concat_axis=0, tiled=True)  17.7 us
    all_gather x1, blocking collectives, per_device(): lax.all_gather(grad_pred, 'tensor', axis=0, tiled=True)  13.4 us
    all_to_all x1, waiting for transfers between devices, sent_and_summed(): parts = lax.all_to_all(split_up(shard, dim, size), axis, 0, 0, tiled=True)  12.9 us
    psum x1, blocking collectives, per_device(): loss = lax.psum(jnp.sum(root), 'tensor') / V  11.2 us
  transfers between devices with their start and end apart: 11, of which 8 were waited for; matrix products, arithmetic and copies ran while one was open for 9% of the time, Pallas kernels for 0%

profile of v1, /device:TPU:2, one launch (start us, length us, event | category | flops | bytes accessed | tf_op | source)
XLA Modules:
  0.0 263.3 jit_solution(7427000295795546951)
XLA Ops:
  7.2 0.7 all-gather.6.cloned.1.call-update
  7.9 37.8 %all-gather.6.cloned.1.call-done = bf16[896,1024]{1,0:T(8,128)(2,1)} async-done(((bf16[896,128]{1,0:T(8,128)(2,1)}), bf16[896,1024]{1,0:T(8,128)(2,1)}) %all-gather.6.cloned.1.call-update) | async-done | bytes 1835024 | tf_op jit(solution)/shard_map/all_gather | solution.py:95
  45.7 3.6 %fusion.21 = (bf16[896,128]{1,0:T(8,128)(2,1)}, f32[896,128]{1,0:T(8,128)S(1)}) fusion(bf16[896,1024]{1,0:T(8,128)(2,1)} %all-gather.6.cloned.1.call-done, bf16[1024,128]{1,0:T(8,128)(2,1)} %param.9), kind=kOutput, calls=%fused_computation.23 | convolution fusion | flops 242335744 | bytes 2785280 | tf_op jit(solution)/shard_map/dot_general | solution.py:96
  49.5 32.6 %all-gather.8.cloned.1.call-done = bf16[896,1024]{1,0:T(8,128)(2,1)} async-done(((bf16[896,128]{1,0:T(8,128)(2,1)}), bf16[896,1024]{1,0:T(8,128)(2,1)}) %all-gather.8.cloned.1.call-update) | async-done | bytes 1835024 | tf_op jit(solution)/shard_map/all_gather | solution.py:98
  82.0 3.6 %fusion.24 = (bf16[896,128]{1,0:T(8,128)(2,1)}, f32[896,128]{1,0:T(8,128)S(1)}) fusion(bf16[896,1024]{1,0:T(8,128)(2,1)} %all-gather.8.cloned.1.call-done, bf16[1024,128]{1,0:T(8,128)(2,1)} %param.10), kind=kOutput, calls=%fused_computation.26 | convolution fusion | flops 242335744 | bytes 2785280 | tf_op jit(solution)/shard_map/dot_general | solution.py:99
  86.2 0.6 broadcast_in_dim.85
  86.9 13.3 %all-to-all-start.1 = ((f32[64,1,11]{2,1,0:T(1,128)}), f32[64,1,11]{2,1,0:T(1,128)S(1)}, u32[]{:S(2)}, u32[]{:S(2)}) async-start(f32[64,1,11]{2,1,0:T(1,128)} %broadcast_in_dim.85), calls=%async_computation.1 | async-start | bytes 65536 | tf_op jit(solution)/shard_map/all_to_all | solution.py:15
  105.6 6.5 %all-to-all-done.1 = f32[64,1,11]{2,1,0:T(1,128)S(1)} async-done(((f32[64,1,11]{2,1,0:T(1,128)}), f32[64,1,11]{2,1,0:T(1,128)S(1)}, u32[]{:S(2)}, u32[]{:S(2)}) %all-to-all-start.1) | async-done | bytes 2848 | tf_op jit(solution)/shard_map/all_to_all | solution.py:15
  112.1 5.1 %all-to-all-start.2 = ((bf16[8,44,128]{2,1,0:T(8,128)(2,1)}), bf16[8,44,128]{2,1,0:T(8,128)(2,1)S(1)}, u32[]{:S(2)}, u32[]{:S(2)}) async-start(bf16[8,44,128]{2,1,0:T(8,128)(2,1)} %constant_dynamic-update-slice_fusion), calls=%async_computation.2 | async-start | bytes 196608 | tf_op jit(solution)/shard_map/all_to_all | solution.py:79
  117.2 1.2 all-gather.10.cloned.1.call-done
  118.4 2.3 fusion.48
  120.8 0.7 all-to-all-done.2
  122.2 12.6 %all-to-all-start = ((f32[64,1,11]{2,1,0:T(1,128)}), f32[64,1,11]{2,1,0:T(1,128)S(1)}, u32[]{:S(2)}, u32[]{:S(2)}) async-start(f32[64,1,11]{2,1,0:T(1,128)} %broadcast_in_dim.81), calls=%async_computation | async-start | bytes 65536 | tf_op jit(solution)/shard_map/all_to_all | solution.py:15
  135.5 11.2 %all-to-all-done = f32[64,1,11]{2,1,0:T(1,128)S(1)} async-done(((f32[64,1,11]{2,1,0:T(1,128)}), f32[64,1,11]{2,1,0:T(1,128)S(1)}, u32[]{:S(2)}, u32[]{:S(2)}) %all-to-all-start) | async-done | bytes 2848 | tf_op jit(solution)/shard_map/all_to_all | solution.py:15
  146.7 5.8 %all-to-all-start.4 = ((bf16[8,128,128]{2,1,0:T(8,128)(2,1)}), bf16[8,128,128]{2,1,0:T(8,128)(2,1)S(1)}, u32[]{:S(2)}, u32[]{:S(2)}) async-start(bf16[8,128,128]{2,1,0:T(8,128)(2,1)} %bitcast.11), calls=%async_computation.4 | async-start | bytes 524288 | tf_op jit(solution)/shard_map/all_to_all | solution.py:76
  152.9 13.4 %all-gather = bf16[8,44,896]{2,1,0:T(8,128)(2,1)S(1)} all-gather(bf16[1,44,896]{2,1,0:T(8,128)(2,1)S(1)} %bitcast.78), channel_id=1, replica_groups=mesh['space'=64,'tensor'=8] {'tensor'}, dimensions={0}, use_global_device_ids=true | all-gather | bytes 709632 | tf_op jit(solution)/shard_map/all_gather | solution.py:114
  167.1 27.5 %all_to_all.67 = bf16[8,896,128]{2,1,0:T(8,128)(2,1)S(1)} all-to-all(bf16[8,896,128]{2,1,0:T(8,128)(2,1)S(1)} %broadcast_in_dim.86), channel_id=1, replica_groups=mesh['space'=64,'tensor'=8] {'tensor'}, dimensions={0} | all-to-all | bytes 3670016 | tf_op jit(solution)/shard_map/all_to_all | solution.py:15
  194.6 1.3 fusion.13
  195.9 4.8 %all-to-all-start.5 = ((bf16[8,128,128]{2,1,0:T(8,128)(2,1)}), bf16[8,128,128]{2,1,0:T(8,128)(2,1)S(1)}, u32[]{:S(2)}, u32[]{:S(2)}) async-start(bf16[8,128,128]{2,1,0:T(8,128)(2,1)} %bitcast.14), calls=%async_computation.5 | async-start | bytes 524288 | tf_op jit(solution)/shard_map/all_to_all | solution.py:75
  200.7 2.5 copy.43
  203.2 2.6 fusion.7
  206.2 1.2 reshape.130
  207.4 2.2 convolution_convert_fusion.1
  209.6 4.8 %all-to-all-start.7 = ((f32[64,1,704]{2,1,0:T(1,128)}), f32[64,1,704]{2,1,0:T(1,128)S(1)}, u32[]{:S(2)}, u32[]{:S(2)}) async-start(f32[64,1,704]{2,1,0:T(1,128)} %reshape.130), calls=%async_computation.7 | async-start | bytes 393216 | tf_op jit(solution)/shard_map/all_to_all | solution.py:30
  215.0 0.9 pad_maximum_fusion
  215.9 12.9 %all-to-all-done.7 = f32[64,1,704]{2,1,0:T(1,128)S(1)} async-done(((f32[64,1,704]{2,1,0:T(1,128)}), f32[64,1,704]{2,1,0:T(1,128)S(1)}, u32[]{:S(2)}, u32[]{:S(2)}) %all-to-all-start.7) | async-done | bytes 180256 | tf_op jit(solution)/shard_map/all_to_all | solution.py:30
  228.8 4.6 %all-to-all-start.6 = ((bf16[64,16,256]{2,1,0:T(8,128)(2,1)}), bf16[64,16,256]{2,1,0:T(8,128)(2,1)S(1)}, u32[]{:S(2)}, u32[]{:S(2)}) async-start(bf16[64,16,256]{2,1,0:T(8,128)(2,1)} %pad_maximum_fusion), calls=%async_computation.6 | async-start | bytes 1048576 | tf_op jit(solution)/shard_map/all_to_all | solution.py:47
  234.2 11.2 %psum.7 = f32[]{:T(128)} all-reduce(f32[]{:T(128)} %reduce_sum.76), channel_id=1, replica_groups=mesh['space'=64,'tensor'=8] {'tensor'}, use_global_device_ids=true, to_apply=%region_6.7 | all-reduce | flops 1 | bytes 8 | tf_op jit(solution)/shard_map/psum | solution.py:109
  246.6 1.1 reduce.4
  248.1 0.7 bitcast_reduce_fusion
  248.8 3.2 %all-to-all-done.6 = bf16[64,16,256]{2,1,0:T(8,128)(2,1)S(1)} async-done(((bf16[64,16,256]{2,1,0:T(8,128)(2,1)}), bf16[64,16,256]{2,1,0:T(8,128)(2,1)S(1)}, u32[]{:S(2)}, u32[]{:S(2)}) %all-to-all-start.6) | async-done | bytes 524320 | tf_op jit(solution)/shard_map/all_to_all | solution.py:47
  252.7 2.9 %fusion.53 = f32[896,128]{1,0:T(8,128)} fusion(bf16[896,1024]{1,0:T(8,128)(2,1)} %all-gather.12.cloned.1.call-done, bf16[128,1024]{0,1:T(8,128)(2,1)S(1)} %bitcast.74), kind=kOutput, calls=%fused_computation.98 | convolution fusion | flops 234881024 | bytes 2555904 | tf_op jit(solution)/shard_map/dot_general | solution.py:57
  (70 shorter events, 11.5 us)
Async XLA Ops:
  7.2 38.6 %all-gather.6.cloned.1.call-start = ((), (), s32[]{:S(2)}) async-start(), calls=%async_computation.8 | async-start | bytes 2064384 | tf_op jit(solution)/shard_map/all_gather | solution.py:95
  7.9 74.1 %all-gather.8.cloned.1.call-start = ((), (), s32[]{:S(2)}) async-start(), calls=%async_computation.9 | async-start | bytes 2064384 | tf_op jit(solution)/shard_map/all_gather | solution.py:98
  49.4 36.3 %copy-start.5 = (s32[4,896]{1,0:T(4,128)S(1)}, s32[4,896]{1,0:T(4,128)}, u32[]{:S(2)}) copy-start(s32[4,896]{1,0:T(4,128)} %param.13) | copy-start | bytes 43012
  49.4 36.4 %copy-start.6 = (s32[11]{0:T(128)S(1)}, s32[11]{0:T(128)}, u32[]{:S(2)}) copy-start(s32[11]{0:T(128)} %param.14) | copy-start | bytes 136
  49.4 50.8 %copy-start.3 = (bf16[44,1024]{1,0:T(8,128)(2,1)S(1)}, bf16[44,1024]{1,0:T(8,128)(2,1)}, u32[]{:S(2)}) copy-start(bf16[44,1024]{1,0:T(8,128)(2,1)} %param.11) | copy-start | bytes 270340
  49.4 69.0 %all-gather.10.cloned.1.call-start = ((), (), s32[]{:S(2)}) async-start(), calls=%async_computation.10 | async-start | bytes 2064384 | tf_op jit(solution)/shard_map/all_gather | solution.py:101
  85.7 32.7 %copy-start.4 = (f32[44,896]{1,0:T(8,128)S(1)}, f32[44,896]{1,0:T(8,128)}, u32[]{:S(2)}) copy-start(f32[44,896]{1,0:T(8,128)} %param.12) | copy-start | bytes 473092
  86.9 25.3 %all-to-all-start.1 = ((f32[64,1,11]{2,1,0:T(1,128)}), f32[64,1,11]{2,1,0:T(1,128)S(1)}, u32[]{:S(2)}, u32[]{:S(2)}) async-start(f32[64,1,11]{2,1,0:T(1,128)} %broadcast_in_dim.85), calls=%async_computation.1 | async-start | bytes 65536 | tf_op jit(solution)/shard_map/all_to_all | solution.py:15
  112.1 9.4 %all-to-all-start.2 = ((bf16[8,44,128]{2,1,0:T(8,128)(2,1)}), bf16[8,44,128]{2,1,0:T(8,128)(2,1)S(1)}, u32[]{:S(2)}, u32[]{:S(2)}) async-start(bf16[8,44,128]{2,1,0:T(8,128)(2,1)} %constant_dynamic-update-slice_fusion), calls=%async_computation.2 | async-start | bytes 196608 | tf_op jit(solution)/shard_map/all_to_all | solution.py:79
  122.2 24.5 %all-to-all-start = ((f32[64,1,11]{2,1,0:T(1,128)}), f32[64,1,11]{2,1,0:T(1,128)S(1)}, u32[]{:S(2)}, u32[]{:S(2)}) async-start(f32[64,1,11]{2,1,0:T(1,128)} %broadcast_in_dim.81), calls=%async_computation | async-start | bytes 65536 | tf_op jit(solution)/shard_map/all_to_all | solution.py:15
  146.7 20.1 %all-to-all-start.4 = ((bf16[8,128,128]{2,1,0:T(8,128)(2,1)}), bf16[8,128,128]{2,1,0:T(8,128)(2,1)S(1)}, u32[]{:S(2)}, u32[]{:S(2)}) async-start(bf16[8,128,128]{2,1,0:T(8,128)(2,1)} %bitcast.11), calls=%async_computation.4 | async-start | bytes 524288 | tf_op jit(solution)/shard_map/all_to_all | solution.py:76
  152.5 100.2 %all-gather.12.cloned.1.call-start = ((), (), s32[]{:S(2)}) async-start(), calls=%async_computation.11 | async-start | bytes 2064384 | tf_op jit(solution)/shard_map/all_gather | solution.py:137
  194.6 6.2 %copy-start = (bf16[896,1024]{1,0:T(8,128)(2,1)S(1)}, bf16[896,1024]{1,0:T(8,128)(2,1)}, u32[]{:S(2)}) copy-start(bf16[896,1024]{1,0:T(8,128)(2,1)} %all-gather.10.cloned.1.call-done) | copy-start | bytes 5505028
  195.9 13.6 %all-to-all-start.5 = ((bf16[8,128,128]{2,1,0:T(8,128)(2,1)}), bf16[8,128,128]{2,1,0:T(8,128)(2,1)S(1)}, u32[]{:S(2)}, u32[]{:S(2)}) async-start(bf16[8,128,128]{2,1,0:T(8,128)(2,1)} %bitcast.14), calls=%async_computation.5 | async-start | bytes 524288 | tf_op jit(solution)/shard_map/all_to_all | solution.py:75
  206.1 8.2 %copy-start.1 = (bf16[896,1024]{1,0:T(8,128)(2,1)S(1)}, bf16[896,1024]{1,0:T(8,128)(2,1)}, u32[]{:S(2)}) copy-start(bf16[896,1024]{1,0:T(8,128)(2,1)} %all-gather.6.cloned.1.call-done) | copy-start | bytes 5505028
  206.1 8.2 %copy-start.2 = (bf16[896,128]{1,0:T(8,128)(2,1)S(1)}, bf16[896,128]{1,0:T(8,128)(2,1)}, u32[]{:S(2)}) copy-start(bf16[896,128]{1,0:T(8,128)(2,1)} %fusion.13) | copy-start | bytes 688132
  209.6 19.2 %all-to-all-start.7 = ((f32[64,1,704]{2,1,0:T(1,128)}), f32[64,1,704]{2,1,0:T(1,128)S(1)}, u32[]{:S(2)}, u32[]{:S(2)}) async-start(f32[64,1,704]{2,1,0:T(1,128)} %reshape.130), calls=%async_computation.7 | async-start | bytes 393216 | tf_op jit(solution)/shard_map/all_to_all | solution.py:30
  228.8 23.2 %all-to-all-start.6 = ((bf16[64,16,256]{2,1,0:T(8,128)(2,1)}), bf16[64,16,256]{2,1,0:T(8,128)(2,1)S(1)}, u32[]{:S(2)}, u32[]{:S(2)}) async-start(bf16[64,16,256]{2,1,0:T(8,128)(2,1)} %pad_maximum_fusion), calls=%async_computation.6 | async-start | bytes 1048576 | tf_op jit(solution)/shard_map/all_to_all | solution.py:47
Sparse Core Ops, SparseCore 0:
  10.1 35.5 all-gather.5
  49.5 32.4 all-gather.7
  85.8 32.5 all-gather.9
  196.1 23.8 all-gather.11
